TPU v7x, 32 devices: a whole 2x2x4 slice. The times are simulated.
32 devices in a mesh: seq: 8 (over z, x), chan: 4 (over y, core).
Axes of the slice: x: 2, y: 2, z: 4, core: 2. Of those that a mesh axis runs over, the one named last changes fastest.
Arguments:
- inputs: bfloat16 [1024, 2048], P('seq', 'chan'), may hold values from -6 to 6
- gate_branch: bfloat16 [1024, 2048], P('seq', 'chan'), may hold values from -6 to 6
- short_taps: float32 [4, 2048], P(None, 'chan'), may hold values from -3 to 3
- filters: float32 [1024, 2048], P('seq', 'chan'), may hold values from -0.1875 to 0.1875
- w_out: bfloat16 [2048, 2048], P('chan'), may hold values from -0.125 to 0.125
- cotangent: bfloat16 [1024, 2048], P('seq', 'chan'), may hold values from -6 to 6
Outputs:
- output: bfloat16 [1024, 2048], P('seq', 'chan')
- grad_inputs: bfloat16 [1024, 2048], P('seq', 'chan')
- grad_gate: bfloat16 [1024, 2048], P('seq', 'chan')
- grad_filters: float32 [1024, 2048], P('seq', 'chan')
- grad_taps: float32 [4, 2048], P(None, 'chan')
- grad_wout: float32 [2048, 2048], P('chan', 'seq')
All inputs are finite; a program needn't handle non-finite values.
Results may differ from a plain program's by a relative error of at most 0.0047.
The roundings to bfloat16 on the way count: a program that leaves them out, or rounds other values in their place, can miss the bound.
Values may be sent and summed in bfloat16 or wider, within the bound.
A program may use at most 64 MiB of HBM per device.

v0:
```python
import math

import functools

import jax
import jax.numpy as jnp
import numpy as np
from jax import lax
from jax.experimental import pallas as pl
from jax.experimental.pallas import tpu as pltpu
from jax.sharding import PartitionSpec as P

HIGHEST = lax.Precision.HIGHEST


def from_behind(value, axis, steps):
    count = lax.axis_size(axis)
    first, last = (max(0, -steps), min(count, count - steps))
    return lax.ppermute(value, axis, [(source, source + steps) for source in range(first, last)])


def angle_table(row_len, col_len, modulus, row_start, col_start, direction):
    row_ids = lax.iota(jnp.int32, row_len)[:, None] + row_start
    col_ids = lax.iota(jnp.int32, col_len)[None, :] + col_start
    phase = row_ids * col_ids % modulus
    angles = phase.astype(jnp.float32) * (direction * 2.0 * math.pi / modulus)
    return (jnp.cos(angles), jnp.sin(angles))


def column_dft(real_part, imag_part, length, form, direction):
    cos_table, sin_table = angle_table(length, length, length, 0, 0, direction)
    new_real = jnp.einsum(form, real_part, cos_table, precision=HIGHEST) - jnp.einsum(
        form, imag_part, sin_table, precision=HIGHEST
    )
    new_imag = jnp.einsum(form, real_part, sin_table, precision=HIGHEST) + jnp.einsum(
        form, imag_part, cos_table, precision=HIGHEST
    )
    return (new_real, new_imag)


def panel_forward(signal):
    stack_size = signal.shape[0]
    block_len = signal.shape[1]
    part_count = lax.axis_size("seq")
    my_index = lax.axis_index("seq")
    narrow = block_len // part_count
    row_order = 2 * part_count
    full_len = row_order * block_len
    by_column = lax.all_to_all(signal[:, None], "seq", split_axis=2, concat_axis=1, tiled=True)
    row_cos, row_sin = angle_table(row_order, part_count, row_order, 0, 0, -1.0)
    real_part = jnp.einsum("ja,kabf->kjbf", row_cos, by_column, precision=HIGHEST)
    imag_part = jnp.einsum("ja,kabf->kjbf", row_sin, by_column, precision=HIGHEST)
    twist_cos, twist_sin = angle_table(row_order, narrow, full_len, 0, my_index * narrow, -1.0)
    twist_cos = twist_cos[None, :, :, None]
    twist_sin = twist_sin[None, :, :, None]
    real_twist = real_part * twist_cos - imag_part * twist_sin
    imag_twist = real_part * twist_sin + imag_part * twist_cos
    by_rows = lax.all_to_all(
        jnp.concatenate([real_twist, imag_twist], 0), "seq", split_axis=1, concat_axis=2, tiled=True
    )
    return column_dft(by_rows[:stack_size], by_rows[stack_size:], block_len, "kjbf,bm->kjmf", -1.0)


def panel_inverse(real_part, imag_part):
    stack_size = real_part.shape[0]
    block_len = real_part.shape[2]
    part_count = lax.axis_size("seq")
    my_index = lax.axis_index("seq")
    row_order = 2 * part_count
    full_len = row_order * block_len
    real_back, imag_back = column_dft(real_part, imag_part, block_len, "kjmf,mb->kjbf", 1.0)
    twist_cos, twist_sin = angle_table(2, block_len, full_len, my_index * 2, 0, 1.0)
    twist_cos = twist_cos[None, :, :, None]
    twist_sin = twist_sin[None, :, :, None]
    real_twist = (real_back * twist_cos - imag_back * twist_sin) / block_len
    imag_twist = (real_back * twist_sin + imag_back * twist_cos) / block_len
    by_column = lax.all_to_all(
        jnp.concatenate([real_twist, imag_twist], 0), "seq", split_axis=2, concat_axis=1, tiled=True
    )
    row_cos, row_sin = angle_table(part_count, row_order, row_order, 0, 0, 1.0)
    signal = (
        jnp.einsum("aj,kjbf->kabf", row_cos, by_column[:stack_size], precision=HIGHEST)
        - jnp.einsum("aj,kjbf->kabf", row_sin, by_column[stack_size:], precision=HIGHEST)
    ) / row_order
    returned = lax.all_to_all(signal, "seq", split_axis=1, concat_axis=2, tiled=True)
    return returned[:, 0]


def panel_local(inputs, gate_branch, short_taps, filters, w_out, cotangent):
    forward_fn, inverse_fn = (panel_forward, panel_inverse)
    tap_count = short_taps.shape[0]
    row_count = inputs.shape[0]
    left_tail = from_behind(inputs[row_count - (tap_count - 1) :], "seq", 1)
    extended = jnp.concatenate([left_tail, inputs], 0).astype(jnp.float32)
    mixed = jnp.zeros((row_count, inputs.shape[1]), jnp.float32)
    for tap_index in range(tap_count):
        start_row = tap_count - 1 - tap_index
        mixed = mixed + short_taps[tap_index] * extended[start_row : start_row + row_count]
    spec_real, spec_imag = forward_fn(jnp.stack([mixed, filters], 0))
    mixed_real, filter_real = (spec_real[0], spec_real[1])
    mixed_imag, filter_imag = (spec_imag[0], spec_imag[1])
    prod_real = mixed_real * filter_real - mixed_imag * filter_imag
    prod_imag = mixed_real * filter_imag + mixed_imag * filter_real
    convolved = inverse_fn(prod_real[None], prod_imag[None])[0]
    gate_wide = gate_branch.astype(jnp.float32)
    gated = (gate_wide * convolved).astype(jnp.bfloat16)
    out_terms = jnp.dot(gated, w_out, preferred_element_type=jnp.float32)
    output = lax.psum_scatter(out_terms, "chan", scatter_dimension=1, tiled=True).astype(
        jnp.bfloat16
    )
    full_cot = lax.all_gather(cotangent, "chan", axis=1, tiled=True)
    grad_gated = lax.dot_general(
        full_cot, w_out, (((1,), (1,)), ((), ())), preferred_element_type=jnp.float32
    )
    grad_gate = (grad_gated * convolved).astype(jnp.bfloat16)
    grad_conv = grad_gated * gate_wide
    grad_real, grad_imag = forward_fn(grad_conv[None])
    grad_real = grad_real[0]
    grad_imag = grad_imag[0]
    back_real = jnp.stack(
        [
            filter_real * grad_real + filter_imag * grad_imag,
            mixed_real * grad_real + mixed_imag * grad_imag,
        ],
        0,
    )
    back_imag = jnp.stack(
        [
            filter_real * grad_imag - filter_imag * grad_real,
            mixed_real * grad_imag - mixed_imag * grad_real,
        ],
        0,
    )
    gradients = inverse_fn(back_real, back_imag)
    grad_mixed = gradients[0]
    grad_filters = gradients[1]
    right_head = from_behind(grad_mixed[: tap_count - 1], "seq", -1)
    grad_ext = jnp.concatenate([grad_mixed, right_head], 0)
    grad_wide = jnp.zeros_like(grad_mixed)
    tap_rows = []
    for tap_index in range(tap_count):
        start_row = tap_count - 1 - tap_index
        grad_wide = grad_wide + short_taps[tap_index] * grad_ext[tap_index : tap_index + row_count]
        tap_rows.append(jnp.sum(extended[start_row : start_row + row_count] * grad_mixed, axis=0))
    grad_inputs = grad_wide.astype(jnp.bfloat16)
    grad_taps = lax.psum(jnp.stack(tap_rows, 0), "seq")
    weight_terms = lax.dot_general(
        gated, full_cot, (((0,), (0,)), ((), ())), preferred_element_type=jnp.float32
    )
    grad_wout = lax.psum_scatter(weight_terms, "seq", scatter_dimension=1, tiled=True)
    return (output, grad_inputs, grad_gate, grad_filters, grad_taps, grad_wout)


DENSE_TOKENS = 2048


def split_table(table):
    high = table.astype(jnp.bfloat16)
    low = (table - high.astype(np.float64)).astype(jnp.bfloat16)
    return (high, low)


def dense_tables(tokens):
    freq = np.arange(tokens, dtype=np.int64)[:, None]
    time = np.arange(tokens, dtype=np.int64)[None, :]
    angles = ((2 * freq + 1) * time % (4 * tokens)) * (2.0 * np.pi / (4 * tokens))
    forward = np.concatenate([np.cos(angles), -np.sin(angles)], 0)
    inverse = forward.T / tokens
    return (split_table(forward), split_table(inverse))


LANES = 128
HALF = 64
TILE = 256
BF16 = jnp.bfloat16
F32 = jnp.float32


def left_half(shape):
    return lax.broadcasted_iota(jnp.int32, shape, 1) < HALF


def turned(value):
    return pltpu.roll(value, HALF, 1)


def split_value(value):
    high = value.astype(BF16)
    return (high, (value - high.astype(F32)).astype(BF16))


def packed_split(value):
    high = value.astype(BF16).astype(F32)
    return jnp.where(left_half(value.shape), high, value - high).astype(BF16)


def tiles(count, body):
    def step(index, carry):
        body(pl.ds(pl.multiple_of(index * TILE, TILE), TILE))
        return carry

    lax.fori_loop(0, count // TILE, step, 0)


def product(left, right):
    return jnp.dot(left, right, preferred_element_type=F32)


def wide_transform(high, low, value, result):
    def body(rows):
        first = product(high[rows, :], value[...])
        second = product(low[rows, :], value[:, :LANES])
        result[rows, :] = first[:, :LANES] + first[:, LANES:] + second

    tiles(result.shape[0], body)


def half_transform(high, low, value, result):
    def body(rows):
        total = product(high[rows, :], value[...]) + product(low[rows, :], value[...])
        result[rows, :] = total + turned(total)

    tiles(result.shape[0], body)


def moved(value, steps):
    if steps == 0:
        return value
    count = value.shape[0]
    row = lax.broadcasted_iota(jnp.int32, value.shape, 0)
    keep = (row >= steps) if steps > 0 else (row < count + steps)
    return jnp.where(keep, pltpu.roll(value, steps % count, 0), 0.0)


def block_kernel(
    inputs, gate, taps, filters, w_out, cot, fwd_high_hbm, fwd_low_hbm, inv_high_hbm, inv_low_hbm,
    output, grad_inputs, grad_gate, grad_filters, grad_taps, grad_wout,
    fwd_high, fwd_low, inv_high, inv_low, cot_all, cot_send, cot_cols, first_send, first_got,
    second_send, second_got, gated_all, third_send, third_got, gate_send, gate_got,
    taps_send, taps_got, part_send, part_got, wide_short, half_short, half_long, wide_long,
    spec, grad_spec, signal, mixing, table_sems, send_sems, recv_sems, chan_send_sems, chan_recv_sems,
):
    parts, rows = first_got.shape[0], first_got.shape[1]
    chans, cols = cot_all.shape[0], inputs.shape[1]
    tokens = parts * rows
    tap_count = taps.shape[0]
    me = lax.axis_index("seq")
    mine = lax.axis_index("chan")

    tables = [
        pltpu.make_async_copy(source, target, table_sems.at[index])
        for index, (source, target) in enumerate(
            [
                (fwd_high_hbm, fwd_high), (fwd_low_hbm, fwd_low),
                (inv_high_hbm, inv_high), (inv_low_hbm, inv_low),
            ]
        )
    ]
    for table in tables:
        table.start()

    barrier = pltpu.get_barrier_semaphore()
    for step in range(1, parts):
        pl.semaphore_signal(
            barrier, inc=1, device_id=(lax.rem(me + step, parts), mine),
            device_id_type=pl.DeviceIdType.MESH,
        )
    for step in range(1, chans):
        pl.semaphore_signal(
            barrier, inc=1, device_id=(me, lax.rem(mine + step, chans)),
            device_id_type=pl.DeviceIdType.MESH,
        )
    pl.semaphore_wait(barrier, parts + chans - 2)

    def to_seq(kind, step, source, target):
        return pltpu.make_async_remote_copy(
            src_ref=source, dst_ref=target,
            send_sem=send_sems.at[kind, step], recv_sem=recv_sems.at[kind, step],
            device_id=(lax.rem(me + step, parts), mine), device_id_type=pl.DeviceIdType.MESH,
        )

    def to_chan(kind, step, source, target):
        return pltpu.make_async_remote_copy(
            src_ref=source, dst_ref=target,
            send_sem=chan_send_sems.at[kind, step], recv_sem=chan_recv_sems.at[kind, step],
            device_id=(me, lax.rem(mine + step, chans)), device_id_type=pl.DeviceIdType.MESH,
        )

    def launch(copies):
        for copy in copies:
            copy.start()
        return copies

    def arrive(copies):
        for copy in copies:
            copy.wait_recv()

    def exchange(kind, sent, got):
        copies = launch(
            [
                to_seq(kind, step, sent.at[lax.rem(me + step, parts)], got.at[me])
                for step in range(1, parts)
            ]
        )
        got[pl.ds(me, 1)] = sent[pl.ds(me, 1)]
        return copies

    def pack(left, right, target):
        for pair in range(parts // 2):
            span = slice(pair * LANES, (pair + 1) * LANES)
            a, b = (left[:, span].astype(F32), right[:, span].astype(F32))
            low = left_half(a.shape)
            target[2 * pair] = jnp.where(low, a, turned(b)).astype(BF16)
            target[2 * pair + 1] = jnp.where(low, turned(a), b).astype(BF16)

    cot_copies = launch([to_chan(0, step, cot, cot_all.at[mine]) for step in range(1, chans)])
    cot_all[pl.ds(mine, 1)] = cot[...][None]
    pack(inputs, filters, first_send)
    first_copies = exchange(0, first_send, first_got)

    arrive(cot_copies)
    grad_gated = jnp.zeros((rows, cols), F32)
    for chan in range(chans):
        grad_gated = grad_gated + lax.dot_general(
            cot_all[chan], w_out[:, chan * cols : (chan + 1) * cols],
            (((1,), (1,)), ((), ())), preferred_element_type=F32,
        )
    pack(gate, grad_gated, second_send)
    second_copies = exchange(1, second_send, second_got)
    share = chans * cols // parts
    for part in range(parts):
        chan, start = divmod(part * share, cols)
        cot_send[part] = cot_all[chan, :, start : start + share]
    cot_col_copies = exchange(2, cot_send, cot_cols)

    own_taps = taps[:, pl.ds(pl.multiple_of(lax.div(me, 2) * LANES, LANES), LANES)]
    odd = jnp.full(own_taps.shape, lax.rem(me, 2), jnp.int32) == 1
    own_taps = jnp.where(odd, turned(own_taps), own_taps)
    tap_ids = lax.broadcasted_iota(jnp.int32, own_taps.shape, 0)
    mixing[...] = jnp.where(left_half(own_taps.shape), own_taps, (tap_ids == 0).astype(F32))

    arrive(first_copies)
    packed = first_got[...].reshape(tokens, LANES).astype(F32)
    mixed = packed * mixing[0:1, :]
    for tap in range(1, tap_count):
        mixed = mixed + mixing[tap : tap + 1, :] * moved(packed, tap)
    high, low = split_value(mixed)
    wide_short[:, :LANES] = high
    wide_short[:, LANES:] = low
    for table in tables:
        table.wait()
    wide_transform(fwd_high, fwd_low, wide_short, spec)

    def multiply(rows_at):
        other = pl.ds(pl.multiple_of(rows_at.start + tokens, TILE), TILE)
        real, imag = (spec[rows_at, :], spec[other, :])
        real_turned, imag_turned = (turned(real), turned(imag))
        half_long[rows_at, :] = packed_split(real * real_turned - imag * imag_turned)
        half_long[other, :] = packed_split(real * imag_turned + imag * real_turned)

    tiles(tokens, multiply)
    half_transform(inv_high, inv_low, half_long, signal)

    arrive(second_copies)
    for part in range(parts):
        span = slice(part * rows, (part + 1) * rows)
        branch = second_got[part].astype(F32)
        scaled = branch * signal[span, :]
        gated_all[pl.ds(me, 1), :, span] = scaled.T[:HALF].astype(BF16)[None]
        gate_send[part] = jnp.where(
            left_half((rows // 2, LANES)), turned(scaled[: rows // 2]), scaled[rows // 2 :]
        ).astype(BF16)
        half_short[span, :] = packed_split(branch * turned(branch))

    line = [
        to_seq(3, step, gated_all.at[me], gated_all.at[me]) for step in range(1, parts)
    ]
    launch(line)
    gate_copies = exchange(4, gate_send, gate_got)

    half_transform(fwd_high, fwd_low, half_short, grad_spec)

    def back(rows_at):
        other = pl.ds(pl.multiple_of(rows_at.start + tokens, TILE), TILE)
        real, imag = (turned(spec[rows_at, :]), turned(spec[other, :]))
        grad_real, grad_imag = (grad_spec[rows_at, :], grad_spec[other, :])
        high, low = split_value(real * grad_real + imag * grad_imag)
        wide_long[rows_at, :LANES] = high
        wide_long[rows_at, LANES:] = low
        high, low = split_value(real * grad_imag - imag * grad_real)
        wide_long[other, :LANES] = high
        wide_long[other, LANES:] = low

    tiles(tokens, back)
    wide_transform(inv_high, inv_low, wide_long, signal)
    grads = signal[...]
    mixed_back = grads * mixing[0:1, :]
    packed = first_got[...].reshape(tokens, LANES).astype(F32)
    taps_send[...] = jnp.zeros_like(taps_send)
    for tap in range(tap_count):
        if tap:
            mixed_back = mixed_back + mixing[tap : tap + 1, :] * moved(grads, -tap)
        taps_send[tap : tap + 1, :] = jnp.sum(
            moved(packed, tap) * grads, axis=0, keepdims=True
        )
    third_send[...] = mixed_back.astype(BF16).reshape(parts, rows, LANES)
    third_copies = exchange(5, third_send, third_got)
    taps_copies = launch(
        [to_seq(6, step, taps_send, taps_got.at[me]) for step in range(1, parts)]
    )
    taps_got[pl.ds(me, 1)] = taps_send[...][None]

    arrive(line)
    here = pl.ds(pl.multiple_of(me * rows, rows), rows)
    own_gated = gated_all[:, :, here].astype(F32).reshape(parts * HALF, rows).T.astype(BF16)
    for chan in range(chans):
        part_send[chan] = product(own_gated, w_out[:, chan * cols : (chan + 1) * cols]).astype(BF16)
    part_copies = launch(
        [
            to_chan(1, step, part_send.at[lax.rem(mine + step, chans)], part_got.at[mine])
            for step in range(1, chans)
        ]
    )
    part_got[pl.ds(mine, 1)] = part_send[pl.ds(mine, 1)]

    arrive(cot_col_copies)
    grad_wout[...] = product(
        gated_all[...].reshape(parts * HALF, tokens), cot_cols[...].reshape(tokens, share)
    )
    arrive(gate_copies)
    arrive(third_copies)
    arrive(taps_copies)
    for pair in range(parts // 2):
        span = slice(pair * LANES, (pair + 1) * LANES)
        a, b = (third_got[2 * pair].astype(F32), third_got[2 * pair + 1].astype(F32))
        low = left_half(a.shape)
        grad_inputs[:, span] = jnp.where(low, a, turned(b)).astype(BF16)
        grad_filters[:, span] = jnp.where(low, turned(a), b)
        a, b = (gate_got[2 * pair].astype(F32), gate_got[2 * pair + 1].astype(F32))
        low = left_half(a.shape)
        grad_gate[: rows // 2, span] = jnp.where(low, a, turned(b)).astype(BF16)
        grad_gate[rows // 2 :, span] = jnp.where(low, turned(a), b).astype(BF16)
        a, b = (taps_got[2 * pair], taps_got[2 * pair + 1])
        grad_taps[:, span] = jnp.where(left_half(a.shape), a, turned(b))[:tap_count]

    arrive(part_copies)
    total = part_got[0].astype(F32)
    for chan in range(1, chans):
        total = total + part_got[chan].astype(F32)
    output[...] = total.astype(BF16)
    for copies in (
        cot_copies, first_copies, second_copies, cot_col_copies, line, gate_copies,
        third_copies, taps_copies, part_copies,
    ):
        for copy in copies:
            copy.wait_send()


def dense_local(inputs, gate_branch, short_taps, filters, w_out, cotangent):
    parts = lax.axis_size("seq")
    chans = lax.axis_size("chan")
    rows, cols = inputs.shape
    tokens = rows * parts
    share = cols * chans // parts
    tap_rows = 8
    (fwd_high, fwd_low), (inv_high, inv_low) = dense_tables(tokens)
    vmem = pl.BlockSpec(memory_space=pltpu.VMEM)
    hbm = pl.BlockSpec(memory_space=pl.ANY)
    shape = jax.ShapeDtypeStruct
    return pl.pallas_call(
        block_kernel,
        out_shape=(
            shape((rows, cols), BF16), shape((rows, cols), BF16), shape((rows, cols), BF16),
            shape((rows, cols), F32), shape(short_taps.shape, F32), shape((cols, share), F32),
        ),
        in_specs=[vmem] * 6 + [hbm] * 4,
        out_specs=[vmem] * 6,
        scratch_shapes=[
            pltpu.VMEM((2 * tokens, tokens), BF16), pltpu.VMEM((2 * tokens, tokens), BF16),
            pltpu.VMEM((tokens, 2 * tokens), BF16), pltpu.VMEM((tokens, 2 * tokens), BF16),
            pltpu.VMEM((chans, rows, cols), BF16),
            pltpu.VMEM((parts, rows, share), BF16), pltpu.VMEM((parts, rows, share), BF16),
            pltpu.VMEM((parts, rows, LANES), BF16), pltpu.VMEM((parts, rows, LANES), BF16),
            pltpu.VMEM((parts, rows, LANES), BF16), pltpu.VMEM((parts, rows, LANES), BF16),
            pltpu.VMEM((parts, HALF, tokens), BF16),
            pltpu.VMEM((parts, rows, LANES), BF16), pltpu.VMEM((parts, rows, LANES), BF16),
            pltpu.VMEM((parts, rows // 2, LANES), BF16), pltpu.VMEM((parts, rows // 2, LANES), BF16),
            pltpu.VMEM((tap_rows, LANES), F32), pltpu.VMEM((parts, tap_rows, LANES), F32),
            pltpu.VMEM((chans, rows, cols), BF16), pltpu.VMEM((chans, rows, cols), BF16),
            pltpu.VMEM((tokens, 2 * LANES), BF16), pltpu.VMEM((tokens, LANES), BF16),
            pltpu.VMEM((2 * tokens, LANES), BF16), pltpu.VMEM((2 * tokens, 2 * LANES), BF16),
            pltpu.VMEM((2 * tokens, LANES), F32), pltpu.VMEM((2 * tokens, LANES), F32),
            pltpu.VMEM((tokens, LANES), F32), pltpu.VMEM((short_taps.shape[0], LANES), F32),
            pltpu.SemaphoreType.DMA((4,)),
            pltpu.SemaphoreType.DMA((7, parts)), pltpu.SemaphoreType.DMA((7, parts)),
            pltpu.SemaphoreType.DMA((2, chans)), pltpu.SemaphoreType.DMA((2, chans)),
        ],
        compiler_params=pltpu.CompilerParams(
            collective_id=0, has_side_effects=True, vmem_limit_bytes=56 * 1024 * 1024
        ),
    )(inputs, gate_branch, short_taps, filters, w_out, cotangent, fwd_high, fwd_low, inv_high, inv_low)


def local(inputs, *others):
    parts = lax.axis_size("seq")
    rows, cols = inputs.shape
    fits = rows * parts <= DENSE_TOKENS and rows % LANES == 0 and cols == HALF * parts
    return (dense_local if fits else panel_local)(inputs, *others)


def solution(mesh):
    in_specs = (
        P("seq", "chan"),
        P("seq", "chan"),
        P(None, "chan"),
        P("seq", "chan"),
        P("chan", None),
        P("seq", "chan"),
    )
    out_specs = (
        P("seq", "chan"),
        P("seq", "chan"),
        P("seq", "chan"),
        P("seq", "chan"),
        P(None, "chan"),
        P("chan", "seq"),
    )
    return jax.shard_map(local, mesh=mesh, in_specs=in_specs, out_specs=out_specs, check_vma=False)
```

profile of v0, /device:TPU:0, one launch (start us, length us, event | category | flops | bytes accessed | tf_op | source)
XLA Modules:
  0.0 77.6 jit_solution(6962076131053305882)
XLA Ops:
  0.6 67.4 %shard_map.145 = (bf16[128,512]{1,0:T(8,128)(2,1)}, bf16[128,512]{1,0:T(8,128)(2,1)}, bf16[128,512]{1,0:T(8,128)(2,1)}, f32[128,512]{1,0:T(8,128)}, f32[4,512]{1,0:T(4,128)}, /*index=5*/f32[512,256]{1,0:T(8,128)}) custom-call(bf16[128,512]{1,0:T(8,128)(2,1)} %inputs.1, bf16[128,512]{1,0:T(8,128)(2,1)} %gate.1, f32[4,512]{1,0:T(4,128)} %taps.1, ...), custom_call_target="tpu_custom_call" | custom-call | tf_op jit(solution)/shard_map/pallas_call | solution.py:470
  68.1 1.6 %copy.22 = bf16[128,512]{1,0:T(8,128)(2,1)} copy(bf16[128,512]{1,0:T(8,128)(2,1)} %get-tuple-element.12) | data formatting | bytes 262144
  69.6 1.6 %copy.23 = bf16[128,512]{1,0:T(8,128)(2,1)} copy(bf16[128,512]{1,0:T(8,128)(2,1)} %get-tuple-element.13) | data formatting | bytes 262144
  71.2 1.6 %copy.24 = bf16[128,512]{1,0:T(8,128)(2,1)} copy(bf16[128,512]{1,0:T(8,128)(2,1)} %get-tuple-element.14) | data formatting | bytes 262144
  72.8 1.7 %copy.25 = f32[128,512]{1,0:T(8,128)} copy(f32[128,512]{1,0:T(8,128)} %get-tuple-element.15) | data formatting | bytes 524288
  74.4 1.3 %copy.26 = f32[4,512]{1,0:T(4,128)} copy(f32[4,512]{1,0:T(4,128)} %get-tuple-element.16) | data formatting | bytes 16384
  75.7 1.9 %copy.27 = f32[512,256]{1,0:T(8,128)} copy(f32[512,256]{1,0:T(8,128)} %get-tuple-element.17) | data formatting | bytes 1048576
where the time goes:
time: 78.5 us; the launch traced here: 77.6 us
  Pallas kernels  67.4 us (86%)
  local copies, waits for them, and re-layouts  9.53 us (12%)
    pallas_call x1, Pallas kernels, dense_local(): pl.pallas_call(block_kernel, out_shape=(shape((rows, cols), BF16), shape(...  67.4 us
    unnamed x6, local copies, waits for them, and re-layouts  9.53 us

commit v1 on v0

--- a/solution.py
+++ b/solution.py
@@ -172,6 +172,7 @@
 LANES = 128
 HALF = 64
 TILE = 256
+DOT_TILE = 512
 BF16 = jnp.bfloat16
 F32 = jnp.float32
 
@@ -194,12 +195,12 @@
     return jnp.where(left_half(value.shape), high, value - high).astype(BF16)
 
 
-def tiles(count, body):
+def tiles(count, body, size=TILE):
     def step(index, carry):
-        body(pl.ds(pl.multiple_of(index * TILE, TILE), TILE))
+        body(pl.ds(pl.multiple_of(index * size, size), size))
         return carry
 
-    lax.fori_loop(0, count // TILE, step, 0)
+    lax.fori_loop(0, count // size, step, 0)
 
 
 def product(left, right):
@@ -212,7 +213,7 @@
         second = product(low[rows, :], value[:, :LANES])
         result[rows, :] = first[:, :LANES] + first[:, LANES:] + second
 
-    tiles(result.shape[0], body)
+    tiles(result.shape[0], body, DOT_TILE)
 
 
 def half_transform(high, low, value, result):
@@ -220,7 +221,7 @@
         total = product(high[rows, :], value[...]) + product(low[rows, :], value[...])
         result[rows, :] = total + turned(total)
 
-    tiles(result.shape[0], body)
+    tiles(result.shape[0], body, DOT_TILE)
 
 
 def moved(value, steps):
@@ -233,10 +234,10 @@
 
 
 def block_kernel(
-    inputs, gate, taps, filters, w_out, cot, fwd_high_hbm, fwd_low_hbm, inv_high_hbm, inv_low_hbm,
+    inputs, gate, taps, filters, w_out_hbm, cot, fwd_high_hbm, fwd_low_hbm, inv_high_hbm, inv_low_hbm,
     output, grad_inputs, grad_gate, grad_filters, grad_taps, grad_wout,
-    fwd_high, fwd_low, inv_high, inv_low, cot_all, cot_send, cot_cols, first_send, first_got,
-    second_send, second_got, gated_all, third_send, third_got, gate_send, gate_got,
+    w_out, fwd_high, fwd_low, inv_high, inv_low, cot_all, cot_send, cot_cols, first_send, first_got,
+    second_send, second_got, gated_all, own_got, third_send, third_got, gate_send, gate_got,
     taps_send, taps_got, part_send, part_got, wide_short, half_short, half_long, wide_long,
     spec, grad_spec, signal, mixing, table_sems, send_sems, recv_sems, chan_send_sems, chan_recv_sems,
 ):
@@ -251,7 +252,7 @@
         pltpu.make_async_copy(source, target, table_sems.at[index])
         for index, (source, target) in enumerate(
             [
-                (fwd_high_hbm, fwd_high), (fwd_low_hbm, fwd_low),
+                (w_out_hbm, w_out), (fwd_high_hbm, fwd_high), (fwd_low_hbm, fwd_low),
                 (inv_high_hbm, inv_high), (inv_low_hbm, inv_low),
             ]
         )
@@ -319,6 +320,7 @@
     first_copies = exchange(0, first_send, first_got)
 
     arrive(cot_copies)
+    tables[0].wait()
     grad_gated = jnp.zeros((rows, cols), F32)
     for chan in range(chans):
         grad_gated = grad_gated + lax.dot_general(
@@ -328,10 +330,20 @@
     pack(gate, grad_gated, second_send)
     second_copies = exchange(1, second_send, second_got)
     share = chans * cols // parts
+    quarter_rows = rows // chans
+    quarter = pl.ds(pl.multiple_of(mine * quarter_rows, quarter_rows), quarter_rows)
     for part in range(parts):
         chan, start = divmod(part * share, cols)
-        cot_send[part] = cot_all[chan, :, start : start + share]
-    cot_col_copies = exchange(2, cot_send, cot_cols)
+        cot_send[part] = cot_all[chan, quarter, start : start + share]
+    cot_col_copies = launch(
+        [
+            to_seq(
+                2, step, cot_send.at[lax.rem(me + step, parts)], cot_cols.at[me, quarter]
+            )
+            for step in range(1, parts)
+        ]
+    )
+    cot_cols[pl.ds(me, 1), quarter] = cot_send[pl.ds(me, 1)]
 
     own_taps = taps[:, pl.ds(pl.multiple_of(lax.div(me, 2) * LANES, LANES), LANES)]
     odd = jnp.full(own_taps.shape, lax.rem(me, 2), jnp.int32) == 1
@@ -347,7 +359,7 @@
     high, low = split_value(mixed)
     wide_short[:, :LANES] = high
     wide_short[:, LANES:] = low
-    for table in tables:
+    for table in tables[1:]:
         table.wait()
     wide_transform(fwd_high, fwd_low, wide_short, spec)
 
@@ -361,6 +373,13 @@
     tiles(tokens, multiply)
     half_transform(inv_high, inv_low, half_long, signal)
 
+    arrive(cot_col_copies)
+    cot_row_copies = launch(
+        [
+            to_chan(2, step, cot_cols.at[:, quarter], cot_cols.at[:, quarter])
+            for step in range(1, chans)
+        ]
+    )
     arrive(second_copies)
     for part in range(parts):
         span = slice(part * rows, (part + 1) * rows)
@@ -372,13 +391,53 @@
         ).astype(BF16)
         half_short[span, :] = packed_split(branch * turned(branch))
 
-    line = [
-        to_seq(3, step, gated_all.at[me], gated_all.at[me]) for step in range(1, parts)
-    ]
-    launch(line)
+    own_copies = launch(
+        [
+            to_seq(
+                7, step,
+                gated_all.at[
+                    me, :, pl.ds(pl.multiple_of(lax.rem(me + step, parts) * rows, rows), rows)
+                ],
+                own_got.at[me],
+            )
+            for step in range(1, parts)
+        ]
+    )
+    here = pl.ds(pl.multiple_of(me * rows, rows), rows)
+    own_got[pl.ds(me, 1)] = gated_all[pl.ds(me, 1), :, here]
+    line = launch(
+        [to_seq(3, step, gated_all.at[me], gated_all.at[me]) for step in range(2, parts, 2)]
+    )
+    partner = me + 1 - 2 * lax.rem(me, 2)
+
+    def hand_on(step):
+        source = lax.rem(me + parts - step, parts)
+        return pltpu.make_async_remote_copy(
+            src_ref=gated_all.at[source], dst_ref=gated_all.at[source],
+            send_sem=send_sems.at[8, step], recv_sem=recv_sems.at[8, step],
+            device_id=(partner, mine), device_id_type=pl.DeviceIdType.MESH,
+        )
+
+    handed = launch([hand_on(0)])
     gate_copies = exchange(4, gate_send, gate_got)
 
     half_transform(fwd_high, fwd_low, half_short, grad_spec)
+
+    arrive(own_copies)
+    own_gated = own_got[...].astype(F32).reshape(parts * HALF, rows).T.astype(BF16)
+    for chan in range(chans):
+        part_send[chan] = product(own_gated, w_out[:, chan * cols : (chan + 1) * cols]).astype(BF16)
+    part_copies = launch(
+        [
+            to_chan(1, step, part_send.at[lax.rem(mine + step, chans)], part_got.at[mine])
+            for step in range(1, chans)
+        ]
+    )
+    part_got[pl.ds(mine, 1)] = part_send[pl.ds(mine, 1)]
+
+    for step, copy in zip(range(2, parts, 2), line):
+        copy.wait_recv()
+        handed += launch([hand_on(step)])
 
     def back(rows_at):
         other = pl.ds(pl.multiple_of(rows_at.start + tokens, TILE), TILE)
@@ -410,20 +469,8 @@
     )
     taps_got[pl.ds(me, 1)] = taps_send[...][None]
 
-    arrive(line)
-    here = pl.ds(pl.multiple_of(me * rows, rows), rows)
-    own_gated = gated_all[:, :, here].astype(F32).reshape(parts * HALF, rows).T.astype(BF16)
-    for chan in range(chans):
-        part_send[chan] = product(own_gated, w_out[:, chan * cols : (chan + 1) * cols]).astype(BF16)
-    part_copies = launch(
-        [
-            to_chan(1, step, part_send.at[lax.rem(mine + step, chans)], part_got.at[mine])
-            for step in range(1, chans)
-        ]
-    )
-    part_got[pl.ds(mine, 1)] = part_send[pl.ds(mine, 1)]
-
-    arrive(cot_col_copies)
+    arrive(cot_row_copies)
+    arrive(handed)
     grad_wout[...] = product(
         gated_all[...].reshape(parts * HALF, tokens), cot_cols[...].reshape(tokens, share)
     )
@@ -449,11 +496,24 @@
         total = total + part_got[chan].astype(F32)
     output[...] = total.astype(BF16)
     for copies in (
-        cot_copies, first_copies, second_copies, cot_col_copies, line, gate_copies,
-        third_copies, taps_copies, part_copies,
+        cot_copies, first_copies, second_copies, cot_col_copies, cot_row_copies, own_copies, line,
+        handed, gate_copies, third_copies, taps_copies, part_copies,
     ):
         for copy in copies:
             copy.wait_send()
+
+
+def store_kernel(*refs):
+    sems = refs[-1]
+    count = sems.shape[0]
+    copies = [
+        pltpu.make_async_copy(refs[index], refs[count + index], sems.at[index])
+        for index in range(count)
+    ]
+    for copy in copies:
+        copy.start()
+    for copy in copies:
+        copy.wait()
 
 
 def dense_local(inputs, gate_branch, short_taps, filters, w_out, cotangent):
@@ -467,22 +527,23 @@
     vmem = pl.BlockSpec(memory_space=pltpu.VMEM)
     hbm = pl.BlockSpec(memory_space=pl.ANY)
     shape = jax.ShapeDtypeStruct
-    return pl.pallas_call(
+    results = pl.pallas_call(
         block_kernel,
         out_shape=(
             shape((rows, cols), BF16), shape((rows, cols), BF16), shape((rows, cols), BF16),
             shape((rows, cols), F32), shape(short_taps.shape, F32), shape((cols, share), F32),
         ),
-        in_specs=[vmem] * 6 + [hbm] * 4,
+        in_specs=[vmem] * 4 + [hbm, vmem] + [hbm] * 4,
         out_specs=[vmem] * 6,
         scratch_shapes=[
+            pltpu.VMEM(w_out.shape, BF16),
             pltpu.VMEM((2 * tokens, tokens), BF16), pltpu.VMEM((2 * tokens, tokens), BF16),
             pltpu.VMEM((tokens, 2 * tokens), BF16), pltpu.VMEM((tokens, 2 * tokens), BF16),
             pltpu.VMEM((chans, rows, cols), BF16),
-            pltpu.VMEM((parts, rows, share), BF16), pltpu.VMEM((parts, rows, share), BF16),
+            pltpu.VMEM((parts, rows // chans, share), BF16), pltpu.VMEM((parts, rows, share), BF16),
             pltpu.VMEM((parts, rows, LANES), BF16), pltpu.VMEM((parts, rows, LANES), BF16),
             pltpu.VMEM((parts, rows, LANES), BF16), pltpu.VMEM((parts, rows, LANES), BF16),
-            pltpu.VMEM((parts, HALF, tokens), BF16),
+            pltpu.VMEM((parts, HALF, tokens), BF16), pltpu.VMEM((parts, HALF, rows), BF16),
             pltpu.VMEM((parts, rows, LANES), BF16), pltpu.VMEM((parts, rows, LANES), BF16),
             pltpu.VMEM((parts, rows // 2, LANES), BF16), pltpu.VMEM((parts, rows // 2, LANES), BF16),
             pltpu.VMEM((tap_rows, LANES), F32), pltpu.VMEM((parts, tap_rows, LANES), F32),
@@ -491,20 +552,29 @@
             pltpu.VMEM((2 * tokens, LANES), BF16), pltpu.VMEM((2 * tokens, 2 * LANES), BF16),
             pltpu.VMEM((2 * tokens, LANES), F32), pltpu.VMEM((2 * tokens, LANES), F32),
             pltpu.VMEM((tokens, LANES), F32), pltpu.VMEM((short_taps.shape[0], LANES), F32),
-            pltpu.SemaphoreType.DMA((4,)),
-            pltpu.SemaphoreType.DMA((7, parts)), pltpu.SemaphoreType.DMA((7, parts)),
-            pltpu.SemaphoreType.DMA((2, chans)), pltpu.SemaphoreType.DMA((2, chans)),
+            pltpu.SemaphoreType.DMA((5,)),
+            pltpu.SemaphoreType.DMA((9, parts)), pltpu.SemaphoreType.DMA((9, parts)),
+            pltpu.SemaphoreType.DMA((3, chans)), pltpu.SemaphoreType.DMA((3, chans)),
         ],
         compiler_params=pltpu.CompilerParams(
             collective_id=0, has_side_effects=True, vmem_limit_bytes=56 * 1024 * 1024
         ),
     )(inputs, gate_branch, short_taps, filters, w_out, cotangent, fwd_high, fwd_low, inv_high, inv_low)
+    count = len(results)
+    return pl.pallas_call(
+        store_kernel,
+        out_shape=[shape(value.shape, value.dtype) for value in results],
+        in_specs=[hbm] * count,
+        out_specs=[hbm] * count,
+        scratch_shapes=[pltpu.SemaphoreType.DMA((count,))],
+    )(*results)
 
 
 def local(inputs, *others):
     parts = lax.axis_size("seq")
     rows, cols = inputs.shape
-    fits = rows * parts <= DENSE_TOKENS and rows % LANES == 0 and cols == HALF * parts
+    fits = rows * parts <= DENSE_TOKENS and rows % LANES == 0 and parts % 2 == 0
+    fits = fits and cols == HALF * parts and rows % (16 * lax.axis_size("chan")) == 0
     return (dense_local if fits else panel_local)(inputs, *others)
 
 

time: 78.5 us -> 94.6 us (1.21)
  Pallas kernels: 67.4 us -> 93.8 us
  local copies, waits for them, and re-layouts: 9.53 us -> 0 us
    pallas_call x0 -> x1, Pallas kernels: none -> 37.1 us  [dense_local(): pl.pallas_call(store_kernel, out_shape=[shape(value.shape, value.dtype) f...]
    pallas_call x1, Pallas kernels: 67.4 us -> 56.6 us  [dense_local(): pl.pallas_call(block_kernel, out_shape=(shape((rows, cols), BF16), shape(...]
    unnamed x6 -> x0, local copies, waits for them, and re-layouts: 9.53 us -> none
where the time goes in v1:
time: 94.6 us; the launch traced here: 94.4 us
  Pallas kernels  93.8 us (99%)
    pallas_call x1, Pallas kernels, dense_local(): pl.pallas_call(block_kernel, out_shape=(shape((rows, cols), BF16), shape(...  56.6 us
    pallas_call x1, Pallas kernels, dense_local(): pl.pallas_call(store_kernel, out_shape=[shape(value.shape, value.dtype) f...  37.1 us

profile of v1, /device:TPU:0, one launch (start us, length us, event | category | flops | bytes accessed | tf_op | source)
XLA Modules:
  0.0 94.4 jit_solution(1340099750852050614)
XLA Ops:
  0.6 56.6 %shard_map.145 = (bf16[128,512]{1,0:T(8,128)(2,1)}, bf16[128,512]{1,0:T(8,128)(2,1)}, bf16[128,512]{1,0:T(8,128)(2,1)}, f32[128,512]{1,0:T(8,128)}, f32[4,512]{1,0:T(4,128)}, /*index=5*/f32[512,256]{1,0:T(8,128)}) custom-call(bf16[128,512]{1,0:T(8,128)(2,1)} %inputs.1, bf16[128,512]{1,0:T(8,128)(2,1)} %gate.1, f32[4,512]{1,0:T(4,128)} %taps.1, ...), custom_call_target="tpu_custom_call" | custom-call | tf_op jit(solution)/shard_map/pallas_call | solution.py:530
  57.3 37.1 %shard_map.146 = (bf16[128,512]{1,0:T(8,128)(2,1)}, bf16[128,512]{1,0:T(8,128)(2,1)}, bf16[128,512]{1,0:T(8,128)(2,1)}, f32[128,512]{1,0:T(8,128)}, f32[4,512]{1,0:T(4,128)}, /*index=5*/f32[512,256]{1,0:T(8,128)}) custom-call(bf16[128,512]{1,0:T(8,128)(2,1)} %get-tuple-element.12.refs_0_, bf16[128,512]{1,0:T(8,128)(2,1)} %get-tuple-element.13.refs_1_, ...), custom_call_target="tpu_custom_call" | custom-call | tf_op jit(solution)/shard_map/pallas_call | solution.py:564

commit v2 on v1

--- a/solution.py
+++ b/solution.py
@@ -319,6 +319,24 @@
     pack(inputs, filters, first_send)
     first_copies = exchange(0, first_send, first_got)
 
+    own_taps = taps[:, pl.ds(pl.multiple_of(lax.div(me, 2) * LANES, LANES), LANES)]
+    odd = jnp.full(own_taps.shape, lax.rem(me, 2), jnp.int32) == 1
+    own_taps = jnp.where(odd, turned(own_taps), own_taps)
+    tap_ids = lax.broadcasted_iota(jnp.int32, own_taps.shape, 0)
+    mixing[...] = jnp.where(left_half(own_taps.shape), own_taps, (tap_ids == 0).astype(F32))
+
+    arrive(first_copies)
+    packed = first_got[...].reshape(tokens, LANES).astype(F32)
+    mixed = packed * mixing[0:1, :]
+    for tap in range(1, tap_count):
+        mixed = mixed + mixing[tap : tap + 1, :] * moved(packed, tap)
+    high, low = split_value(mixed)
+    wide_short[:, :LANES] = high
+    wide_short[:, LANES:] = low
+    tables[1].wait()
+    tables[2].wait()
+    wide_transform(fwd_high, fwd_low, wide_short, spec)
+
     arrive(cot_copies)
     tables[0].wait()
     grad_gated = jnp.zeros((rows, cols), F32)
@@ -345,24 +363,6 @@
     )
     cot_cols[pl.ds(me, 1), quarter] = cot_send[pl.ds(me, 1)]
 
-    own_taps = taps[:, pl.ds(pl.multiple_of(lax.div(me, 2) * LANES, LANES), LANES)]
-    odd = jnp.full(own_taps.shape, lax.rem(me, 2), jnp.int32) == 1
-    own_taps = jnp.where(odd, turned(own_taps), own_taps)
-    tap_ids = lax.broadcasted_iota(jnp.int32, own_taps.shape, 0)
-    mixing[...] = jnp.where(left_half(own_taps.shape), own_taps, (tap_ids == 0).astype(F32))
-
-    arrive(first_copies)
-    packed = first_got[...].reshape(tokens, LANES).astype(F32)
-    mixed = packed * mixing[0:1, :]
-    for tap in range(1, tap_count):
-        mixed = mixed + mixing[tap : tap + 1, :] * moved(packed, tap)
-    high, low = split_value(mixed)
-    wide_short[:, :LANES] = high
-    wide_short[:, LANES:] = low
-    for table in tables[1:]:
-        table.wait()
-    wide_transform(fwd_high, fwd_low, wide_short, spec)
-
     def multiply(rows_at):
         other = pl.ds(pl.multiple_of(rows_at.start + tokens, TILE), TILE)
         real, imag = (spec[rows_at, :], spec[other, :])
@@ -371,6 +371,8 @@
         half_long[other, :] = packed_split(real * imag_turned + imag * real_turned)
 
     tiles(tokens, multiply)
+    tables[3].wait()
+    tables[4].wait()
     half_transform(inv_high, inv_low, half_long, signal)
 
     arrive(cot_col_copies)
@@ -504,16 +506,9 @@
 
 
 def store_kernel(*refs):
-    sems = refs[-1]
-    count = sems.shape[0]
-    copies = [
-        pltpu.make_async_copy(refs[index], refs[count + index], sems.at[index])
-        for index in range(count)
-    ]
-    for copy in copies:
-        copy.start()
-    for copy in copies:
-        copy.wait()
+    count = len(refs) // 2
+    for source, target in zip(refs[:count], refs[count:]):
+        target[...] = source[...]
 
 
 def dense_local(inputs, gate_branch, short_taps, filters, w_out, cotangent):
@@ -564,9 +559,8 @@
     return pl.pallas_call(
         store_kernel,
         out_shape=[shape(value.shape, value.dtype) for value in results],
-        in_specs=[hbm] * count,
-        out_specs=[hbm] * count,
-        scratch_shapes=[pltpu.SemaphoreType.DMA((count,))],
+        in_specs=[vmem] * count,
+        out_specs=[vmem] * count,
     )(*results)
 
 

time: 94.6 us -> 62.5 us (0.66)
  Pallas kernels: 93.8 us -> 61.7 us
    pallas_call x1, Pallas kernels: 37.1 us -> 2.34 us  [dense_local(): pl.pallas_call(store_kernel, out_shape=[shape(value.shape, value.dtype) f...]
    pallas_call x1, Pallas kernels: 56.6 us -> 59.4 us  [dense_local(): pl.pallas_call(block_kernel, out_shape=(shape((rows, cols), BF16), shape(...]
where the time goes in v2:
time: 62.5 us; the launch traced here: 62.4 us
  Pallas kernels  61.7 us (99%)
  between operations  0.64 us (1%)
    pallas_call x1, Pallas kernels, dense_local(): pl.pallas_call(block_kernel, out_shape=(shape((rows, cols), BF16), shape(...  59.4 us
    pallas_call x1, Pallas kernels, dense_local(): pl.pallas_call(store_kernel, out_shape=[shape(value.shape, value.dtype) f...  2.34 us

profile of v2, /device:TPU:0, one launch (start us, length us, event | category | flops | bytes accessed | tf_op | source)
XLA Modules:
  0.0 62.4 jit_solution(15162643450978132290)
XLA Ops:
  0.6 59.4 %shard_map.145 = (bf16[128,512]{1,0:T(8,128)(2,1)}, bf16[128,512]{1,0:T(8,128)(2,1)}, bf16[128,512]{1,0:T(8,128)(2,1)}, f32[128,512]{1,0:T(8,128)}, f32[4,512]{1,0:T(4,128)}, /*index=5*/f32[512,256]{1,0:T(8,128)}) custom-call(bf16[128,512]{1,0:T(8,128)(2,1)} %inputs.1, bf16[128,512]{1,0:T(8,128)(2,1)} %gate.1, f32[4,512]{1,0:T(4,128)} %taps.1, ...), custom_call_target="tpu_custom_call" | custom-call | tf_op jit(solution)/shard_map/pallas_call | solution.py:525
  60.0 2.3 %shard_map.146 = (bf16[128,512]{1,0:T(8,128)(2,1)}, bf16[128,512]{1,0:T(8,128)(2,1)}, bf16[128,512]{1,0:T(8,128)(2,1)}, f32[128,512]{1,0:T(8,128)}, f32[4,512]{1,0:T(4,128)}, /*index=5*/f32[512,256]{1,0:T(8,128)}) custom-call(bf16[128,512]{1,0:T(8,128)(2,1)} %get-tuple-element.12.refs_0_, bf16[128,512]{1,0:T(8,128)(2,1)} %get-tuple-element.13.refs_1_, ...), custom_call_target="tpu_custom_call" | custom-call | tf_op jit(solution)/shard_map/pallas_call | solution.py:559

commit v3 on v2

--- a/solution.py
+++ b/solution.py
@@ -407,21 +407,26 @@
     )
     here = pl.ds(pl.multiple_of(me * rows, rows), rows)
     own_got[pl.ds(me, 1)] = gated_all[pl.ds(me, 1), :, here]
-    line = launch(
-        [to_seq(3, step, gated_all.at[me], gated_all.at[me]) for step in range(2, parts, 2)]
-    )
+    line = [
+        launch(
+            [
+                to_seq(kind, step, gated_all.at[me, span], gated_all.at[me, span])
+                for step in range(2, parts, 2)
+            ]
+        )
+        for kind, span in ((3, slice(0, HALF // 2)), (9, slice(HALF // 2, HALF)))
+    ]
     partner = me + 1 - 2 * lax.rem(me, 2)
 
-    def hand_on(step):
+    def hand_on(kind, step, span):
         source = lax.rem(me + parts - step, parts)
         return pltpu.make_async_remote_copy(
-            src_ref=gated_all.at[source], dst_ref=gated_all.at[source],
-            send_sem=send_sems.at[8, step], recv_sem=recv_sems.at[8, step],
+            src_ref=gated_all.at[source, span], dst_ref=gated_all.at[source, span],
+            send_sem=send_sems.at[kind, step], recv_sem=recv_sems.at[kind, step],
             device_id=(partner, mine), device_id_type=pl.DeviceIdType.MESH,
         )
 
-    handed = launch([hand_on(0)])
-    gate_copies = exchange(4, gate_send, gate_got)
+    handed = launch([hand_on(8, 0, slice(0, HALF))])
 
     half_transform(fwd_high, fwd_low, half_short, grad_spec)
 
@@ -437,9 +442,10 @@
     )
     part_got[pl.ds(mine, 1)] = part_send[pl.ds(mine, 1)]
 
-    for step, copy in zip(range(2, parts, 2), line):
+    for step, copy in zip(range(2, parts, 2), line[0]):
         copy.wait_recv()
-        handed += launch([hand_on(step)])
+        handed += launch([hand_on(8, step, slice(0, HALF // 2))])
+    gate_copies = exchange(4, gate_send, gate_got)
 
     def back(rows_at):
         other = pl.ds(pl.multiple_of(rows_at.start + tokens, TILE), TILE)
@@ -454,6 +460,9 @@
 
     tiles(tokens, back)
     wide_transform(inv_high, inv_low, wide_long, signal)
+    for step, copy in zip(range(2, parts, 2), line[1]):
+        copy.wait_recv()
+        handed += launch([hand_on(10, step, slice(HALF // 2, HALF))])
     grads = signal[...]
     mixed_back = grads * mixing[0:1, :]
     packed = first_got[...].reshape(tokens, LANES).astype(F32)
@@ -498,7 +507,7 @@
         total = total + part_got[chan].astype(F32)
     output[...] = total.astype(BF16)
     for copies in (
-        cot_copies, first_copies, second_copies, cot_col_copies, cot_row_copies, own_copies, line,
+        cot_copies, first_copies, second_copies, cot_col_copies, cot_row_copies, own_copies, *line,
         handed, gate_copies, third_copies, taps_copies, part_copies,
     ):
         for copy in copies:
@@ -548,7 +557,7 @@
             pltpu.VMEM((2 * tokens, LANES), F32), pltpu.VMEM((2 * tokens, LANES), F32),
             pltpu.VMEM((tokens, LANES), F32), pltpu.VMEM((short_taps.shape[0], LANES), F32),
             pltpu.SemaphoreType.DMA((5,)),
-            pltpu.SemaphoreType.DMA((9, parts)), pltpu.SemaphoreType.DMA((9, parts)),
+            pltpu.SemaphoreType.DMA((11, parts)), pltpu.SemaphoreType.DMA((11, parts)),
             pltpu.SemaphoreType.DMA((3, chans)), pltpu.SemaphoreType.DMA((3, chans)),
         ],
         compiler_params=pltpu.CompilerParams(

time: 62.5 us -> 60 us (0.960)
  Pallas kernels: 61.7 us -> 59.2 us
    pallas_call x1, Pallas kernels: 59.4 us -> 56.8 us  [dense_local(): pl.pallas_call(block_kernel, out_shape=(shape((rows, cols), BF16), shape(...]
where the time goes in v3:
time: 60 us; the launch traced here: 59.8 us
  Pallas kernels  59.2 us (99%)
  between operations  0.64 us (1%)
    pallas_call x1, Pallas kernels, dense_local(): pl.pallas_call(block_kernel, out_shape=(shape((rows, cols), BF16), shape(...  56.8 us
    pallas_call x1, Pallas kernels, dense_local(): pl.pallas_call(store_kernel, out_shape=[shape(value.shape, value.dtype) f...  2.34 us

profile of v3, /device:TPU:0, one launch (start us, length us, event | category | flops | bytes accessed | tf_op | source)
XLA Modules:
  0.0 59.8 jit_solution(7795502127189934011)
XLA Ops:
  0.6 56.8 %shard_map.145 = (bf16[128,512]{1,0:T(8,128)(2,1)}, bf16[128,512]{1,0:T(8,128)(2,1)}, bf16[128,512]{1,0:T(8,128)(2,1)}, f32[128,512]{1,0:T(8,128)}, f32[4,512]{1,0:T(4,128)}, /*index=5*/f32[512,256]{1,0:T(8,128)}) custom-call(bf16[128,512]{1,0:T(8,128)(2,1)} %inputs.1, bf16[128,512]{1,0:T(8,128)(2,1)} %gate.1, f32[4,512]{1,0:T(4,128)} %taps.1, ...), custom_call_target="tpu_custom_call" | custom-call | tf_op jit(solution)/shard_map/pallas_call | solution.py:534
  57.5 2.3 %shard_map.146 = (bf16[128,512]{1,0:T(8,128)(2,1)}, bf16[128,512]{1,0:T(8,128)(2,1)}, bf16[128,512]{1,0:T(8,128)(2,1)}, f32[128,512]{1,0:T(8,128)}, f32[4,512]{1,0:T(4,128)}, /*index=5*/f32[512,256]{1,0:T(8,128)}) custom-call(bf16[128,512]{1,0:T(8,128)(2,1)} %get-tuple-element.12.refs_0_, bf16[128,512]{1,0:T(8,128)(2,1)} %get-tuple-element.13.refs_1_, ...), custom_call_target="tpu_custom_call" | custom-call | tf_op jit(solution)/shard_map/pallas_call | solution.py:568

commit v4 on v3

--- a/solution.py
+++ b/solution.py
@@ -172,7 +172,7 @@
 LANES = 128
 HALF = 64
 TILE = 256
-DOT_TILE = 512
+DOT_TILE = 1024
 BF16 = jnp.bfloat16
 F32 = jnp.float32
 

time: 60 us -> 59.6 us (level)
  no operation moved by 1% of the time
where the time goes in v4:
time: 59.6 us; the launch traced here: 59.5 us
  Pallas kernels  58.8 us (99%)
  between operations  0.64 us (1%)
    pallas_call x1, Pallas kernels, dense_local(): pl.pallas_call(block_kernel, out_shape=(shape((rows, cols), BF16), shape(...  56.5 us
    pallas_call x1, Pallas kernels, dense_local(): pl.pallas_call(store_kernel, out_shape=[shape(value.shape, value.dtype) f...  2.34 us

profile of v4, /device:TPU:0, one launch (start us, length us, event | category | flops | bytes accessed | tf_op | source)
XLA Modules:
  0.0 59.5 jit_solution(6920696844165916806)
XLA Ops:
  0.6 56.5 %shard_map.145 = (bf16[128,512]{1,0:T(8,128)(2,1)}, bf16[128,512]{1,0:T(8,128)(2,1)}, bf16[128,512]{1,0:T(8,128)(2,1)}, f32[128,512]{1,0:T(8,128)}, f32[4,512]{1,0:T(4,128)}, /*index=5*/f32[512,256]{1,0:T(8,128)}) custom-call(bf16[128,512]{1,0:T(8,128)(2,1)} %inputs.1, bf16[128,512]{1,0:T(8,128)(2,1)} %gate.1, f32[4,512]{1,0:T(4,128)} %taps.1, ...), custom_call_target="tpu_custom_call" | custom-call | tf_op jit(solution)/shard_map/pallas_call | solution.py:534
  57.1 2.3 %shard_map.146 = (bf16[128,512]{1,0:T(8,128)(2,1)}, bf16[128,512]{1,0:T(8,128)(2,1)}, bf16[128,512]{1,0:T(8,128)(2,1)}, f32[128,512]{1,0:T(8,128)}, f32[4,512]{1,0:T(4,128)}, /*index=5*/f32[512,256]{1,0:T(8,128)}) custom-call(bf16[128,512]{1,0:T(8,128)(2,1)} %get-tuple-element.12.refs_0_, bf16[128,512]{1,0:T(8,128)(2,1)} %get-tuple-element.13.refs_1_, ...), custom_call_target="tpu_custom_call" | custom-call | tf_op jit(solution)/shard_map/pallas_call | solution.py:568
